TPU v7x, 32 devices: a whole 2x2x4 slice. The times are simulated.
32 devices in a mesh: region: 2 (over x), blk: 8 (over z, y), rep: 2 (over core).
Axes of the slice: x: 2, y: 2, z: 4, core: 2. Of those that a mesh axis runs over, the one named last changes fastest.
Arguments:
- readings: bfloat16 [2, 65536, 896], P(None, ('region', 'blk', 'rep')), parts along dimension 1, may hold values from -6 to 6
- tile_mask: int32 [2, 512, 7], P(None, ('region', 'blk', 'rep')), parts along dimension 1, may hold values from 0 to 1, as said below
- sys_factors: float32 [65536, 128], P(('region', 'blk', 'rep')), parts along dimension 0, may hold values from -2 to 2
- sys_first: float32 [65536, 128], P(('region', 'blk', 'rep')), parts along dimension 0, may hold values from -20 to 20
- sys_second: float32 [65536, 128], P(('region', 'blk', 'rep')), parts along dimension 0, may hold values from 10 to 400
- time_factors: float32 [14336, 128], P(('region', 'blk')), parts along dimension 0, may hold values from -2 to 2
- time_first: float32 [14336, 128], P(('region', 'blk')), parts along dimension 0, may hold values from -30 to 30
- time_second: float32 [14336, 128], P(('region', 'blk')), parts along dimension 0, may hold values from 20 to 800
Outputs:
- sys_out: float32 [65536, 128], P(('region', 'blk', 'rep')), parts along dimension 0
- time_out: float32 [14336, 128], P(('region', 'blk')), parts along dimension 0
There are 2 independent parts, one for each index of `region`. A program takes and returns all parts, laid end to end along the dimension named above; each array names one. Nothing has to cross between parts.
Inputs may be any that keep to these rules, and one draw needn't show every extreme that they name: `tile_mask`: 1 where the tile of 128 systems by 128 quarter-hours is observed, else 0.
All inputs are finite; a program needn't handle non-finite values.
Results may differ from a plain program's by a relative error of at most 0.0003.
Values sent between devices are 32-bit elements; how exact they have to be, the bound alone decides.
A program may use at most 128 MiB of HBM per device.

v0:
```python
import jax
import jax.numpy as jnp
from jax import lax
from jax.sharding import PartitionSpec as P

TILE = 128


learn_rate = 0.1
beta_one = 0.8
beta_two = 0.99
adam_eps = 1e-08
decay_weight = 0.01


def passed_along(block, axis, distance):
    devices = range(lax.axis_size(axis))
    route = [((i - distance) % len(devices), i) for i in devices]
    return lax.ppermute(block, axis, route)


def adam_step(param, first, second, grad):
    first_new = beta_one * first + (1.0 - beta_one) * grad
    second_new = beta_two * second + (1.0 - beta_two) * grad * grad
    param_new = param - learn_rate * first_new / (jnp.sqrt(second_new) + adam_eps)
    return (param_new, first_new, second_new)


def residual_grads(sys_rows, time_rows, data, observed):
    sys_low = sys_rows.astype(jnp.bfloat16)
    time_low = time_rows.astype(jnp.bfloat16)
    predict = jnp.dot(sys_low, time_low.T, preferred_element_type=jnp.float32)
    rows, cols = predict.shape
    keep = observed.astype(jnp.float32)[:, None, :, None]
    diff = (predict - data.astype(jnp.float32)).reshape(
        rows // TILE, TILE, cols // TILE, TILE
    ) * keep
    error = diff.reshape(rows, cols).astype(jnp.bfloat16)
    grad_sys = jnp.dot(error, time_low, preferred_element_type=jnp.float32)
    grad_time = lax.dot_general(
        error, sys_low, (((0,), (0,)), ((), ())), preferred_element_type=jnp.float32
    )
    return (grad_sys, grad_time)


def on_device(
    readings, tile_mask, sys_factors, sys_first, sys_second, time_factors, time_first, time_second
):
    rounds = readings.shape[0]
    sys_rows, sys_one, sys_two = (sys_factors, sys_first, sys_second)
    held = time_factors
    held_one, held_two = (time_first, time_second)
    for step in range(rounds):
        grad_sys, part_time = residual_grads(sys_rows, held, readings[step], tile_mask[step])
        grad_time = lax.psum(part_time, "rep")
        sys_rows, sys_one, sys_two = adam_step(
            sys_rows, sys_one, sys_two, grad_sys + decay_weight * sys_rows
        )
        held, held_one, held_two = adam_step(
            held, held_one, held_two, grad_time + decay_weight * held
        )
        if step + 1 < rounds:
            held, held_one, held_two = passed_along((held, held_one, held_two), "blk", 1)
        else:
            held = passed_along(held, "blk", 1)
    return (sys_rows, held)


def solution(mesh):
    return jax.shard_map(
        on_device,
        mesh=mesh,
        in_specs=(
            P(None, ("region", "blk", "rep"), None),
            P(None, ("region", "blk", "rep"), None),
            P(("region", "blk", "rep"), None),
            P(("region", "blk", "rep"), None),
            P(("region", "blk", "rep"), None),
            P(("region", "blk"), None),
            P(("region", "blk"), None),
            P(("region", "blk"), None),
        ),
        out_specs=(P(("region", "blk", "rep"), None), P(("region", "blk"), None)),
        check_vma=False,
    )
```

profile of v0, /device:TPU:0, one launch (start us, length us, event | category | flops | bytes accessed | tf_op | source)
XLA Modules:
  0.0 119.3 jit_solution(7639718747314761473)
XLA Ops:
  7.2 0.0 all-reduce.3.cloned.1.call-start
  7.2 0.8 fusion.29
  8.0 0.5 mul.107
  8.5 6.5 %copy.31 = f32[112,8,16,128]{3,1,2,0:T(8,128)} copy(f32[112,8,16,128]{3,2,1,0:T(8,128)S(1)} %bitcast.28) | data formatting | bytes 14680064
  15.1 8.7 %copy.15 = f32[2048,896]{1,0:T(8,128)} copy(f32[2048,896]{0,1:T(8,128)} %bitcast.29) | data formatting | bytes 14680064 | tf_op jit(solution)/shard_map/mul | solution.py:35
  23.8 5.2 %fusion.3 = bf16[2048,896]{1,0:T(8,128)(2,1)S(1)} fusion(f32[2048,896]{1,0:T(8,128)} %copy.15, bf16[2,2048,896]{2,1,0:T(8,128)(2,1)} %param.8, f32[2048,128]{1,0:T(8,128)S(1)} %copy-done.2, f32[896,128]{1,0:T(8,128)S(1)} %copy-done.3), kind=kOutput, calls=%fused_computation.7 | convolution fusion | flops 477478912 | bytes 16187392 | tf_op jit(solution)/shard_map/dot_general | solution.py:32
  29.0 1.8 %copy-done = bf16[2048,896]{1,0:T(8,128)(2,1)} copy-done((bf16[2048,896]{1,0:T(8,128)(2,1)}, bf16[2048,896]{1,0:T(8,128)(2,1)S(1)}, u32[]{:S(2)}) %copy-start) | copy-done | bytes 3670040
  30.8 1.9 %fusion.19 = f32[896,128]{1,0:T(8,128)} fusion(bf16[2048,896]{1,0:T(8,128)(2,1)S(1)} %fusion.3, f32[2048,128]{1,0:T(8,128)S(1)} %copy-done.2), kind=kOutput, calls=%fused_computation.34 | convolution fusion | flops 470024192 | bytes 5177344 | tf_op jit(solution)/shard_map/dot_general | solution.py:40
  32.7 0.0 all-reduce.3.cloned.1.call-update
  32.8 0.2 all-reduce.5.cloned.1.call-start
  33.0 0.5 mul.124
  33.5 6.6 %copy.30 = f32[112,8,16,128]{3,1,2,0:T(8,128)} copy(f32[112,8,16,128]{3,2,1,0:T(8,128)S(1)} %bitcast.30) | data formatting | bytes 14680064
  40.1 8.7 %copy.17 = f32[2048,896]{1,0:T(8,128)} copy(f32[2048,896]{0,1:T(8,128)} %bitcast.31) | data formatting | bytes 14680064 | tf_op jit(solution)/shard_map/mul | solution.py:35
  48.9 5.4 %all-reduce.3.cloned.1.call-done = f32[896,128]{1,0:T(8,128)} async-done(((f32[896,128]{1,0:T(8,128)}), f32[896,128]{1,0:T(8,128)}) %all-reduce.3.cloned.1.call-update) | async-done | bytes 458768 | tf_op jit(solution)/shard_map/psum | solution.py:55
  54.2 2.2 %divide_subtract_fusion.1 = (f32[896,128]{1,0:T(8,128)S(1)}, f32[896,128]{1,0:T(8,128)}, f32[896,128]{1,0:T(8,128)S(1)}) fusion(f32[896,128]{1,0:T(8,128)S(1)} %copy-done.3, f32[896,128]{1,0:T(8,128)} %all-reduce.3.cloned.1.call-done, f32[896,128]{1,0:T(8,128)S(1)} %copy-done.4, f32[896,128]{1,0:T(8,128)S(1)} %copy-done.5), kind=kLoop, calls=%fused_computation.28 | loop fusion | flops 1490944 | bytes 3211264 | tf_op jit(solution)/shard_map/sub | solution.py:25
  56.5 1.7 %collective-permute-start = (f32[896,128]{1,0:T(8,128)S(1)}, f32[896,128]{1,0:T(8,128)S(1)}, u32[]{:S(2)}, u32[]{:S(2)}) collective-permute-start(f32[896,128]{1,0:T(8,128)S(1)} %get-tuple-element.2), channel_id=1, source_target_pairs={{14,0},{0,2},{2,4},{4,6},{6,8},{8,10},{10,12},{12,14},{15,1},{1,3}... | collective-permute-start | bytes 1376264 | tf_op jit(solution)/shard_map/ppermute | solution.py:19
  58.2 5.9 %divide_subtract_fusion = (f32[2048,128]{1,0:T(8,128)S(1)}, f32[2048,128]{1,0:T(8,128)}) fusion(f32[2048,128]{1,0:T(8,128)S(1)} %copy-done.2, f32[2048,128]{1,0:T(8,128)} %param.11, f32[2048,128]{1,0:T(8,128)} %param.12, bf16[2048,896]{1,0:T(8,128)(2,1)} %copy-done, f32[896,128]{1,0:T(8,128)S(1)} %copy-done.3), kind=kOutput, calls=%fused_computation.18 | convolution fusion | flops 473284608 | bytes 9371648 | tf_op jit(solution)/shard_map/dot_general | solution.py:39
  64.2 1.4 %collective-permute-start.1 = (f32[896,128]{1,0:T(8,128)}, f32[896,128]{1,0:T(8,128)S(1)}, u32[]{:S(2)}, u32[]{:S(2)}) collective-permute-start(f32[896,128]{1,0:T(8,128)} %get-tuple-element.3), channel_id=1, source_target_pairs={{14,0},{0,2},{2,4},{4,6},{6,8},{8,10},{10,12},{12,14},{15,1},{1,3}... | collective-permute-start | bytes 1376264 | tf_op jit(solution)/shard_map/ppermute | solution.py:19
  65.5 1.5 %collective-permute-start.2 = (f32[896,128]{1,0:T(8,128)S(1)}, f32[896,128]{1,0:T(8,128)S(1)}, u32[]{:S(2)}, u32[]{:S(2)}) collective-permute-start(f32[896,128]{1,0:T(8,128)S(1)} %get-tuple-element.4), channel_id=1, source_target_pairs={{14,0},{0,2},{2,4},{4,6},{6,8},{8,10},{10,12},{12,14},{15,1},{1,3}... | collective-permute-start | bytes 1376264 | tf_op jit(solution)/shard_map/ppermute | solution.py:19
  67.0 5.5 %collective-permute-done = f32[896,128]{1,0:T(8,128)S(1)} collective-permute-done((f32[896,128]{1,0:T(8,128)S(1)}, f32[896,128]{1,0:T(8,128)S(1)}, u32[]{:S(2)}, u32[]{:S(2)}) %collective-permute-start) | collective-permute-done | bytes 458784 | tf_op jit(solution)/shard_map/ppermute | solution.py:19
  72.6 1.2 %fusion.1 = bf16[2048,896]{1,0:T(8,128)(2,1)S(1)} fusion(f32[2048,896]{1,0:T(8,128)S(1)} %bitcast.33, bf16[2,2048,896]{2,1,0:T(8,128)(2,1)S(1)} %bitcast.35, f32[2048,128]{1,0:T(8,128)S(1)} %get-tuple-element.7, f32[896,128]{1,0:T(8,128)S(1)} %collective-permute-done), kind=kOutput, calls=%fused_computation.4 | convolution fusion | flops 477478912 | bytes 16187392 | tf_op jit(solution)/shard_map/dot_general | solution.py:32
  73.8 1.8 %copy-done.1 = bf16[2048,896]{1,0:T(8,128)(2,1)} copy-done((bf16[2048,896]{1,0:T(8,128)(2,1)}, bf16[2048,896]{1,0:T(8,128)(2,1)S(1)}, u32[]{:S(2)}) %copy-start.1) | copy-done | bytes 3670040
  75.6 1.9 %fusion.16 = f32[896,128]{1,0:T(8,128)} fusion(bf16[2048,896]{1,0:T(8,128)(2,1)S(1)} %fusion.1, f32[2048,128]{1,0:T(8,128)S(1)} %get-tuple-element.7), kind=kOutput, calls=%fused_computation.31 | convolution fusion | flops 470024192 | bytes 5177344 | tf_op jit(solution)/shard_map/dot_general | solution.py:40
  77.5 0.0 all-reduce.5.cloned.1.call-update
  77.5 4.8 %collective-permute-done.1 = f32[896,128]{1,0:T(8,128)S(1)} collective-permute-done((f32[896,128]{1,0:T(8,128)}, f32[896,128]{1,0:T(8,128)S(1)}, u32[]{:S(2)}, u32[]{:S(2)}) %collective-permute-start.1) | collective-permute-done | bytes 458784 | tf_op jit(solution)/shard_map/ppermute | solution.py:19
  82.4 9.3 %collective-permute-done.2 = f32[896,128]{1,0:T(8,128)S(1)} collective-permute-done((f32[896,128]{1,0:T(8,128)S(1)}, f32[896,128]{1,0:T(8,128)S(1)}, u32[]{:S(2)}, u32[]{:S(2)}) %collective-permute-start.2) | collective-permute-done | bytes 458784 | tf_op jit(solution)/shard_map/ppermute | solution.py:19
  91.6 3.2 %all-reduce.5.cloned.1.call-done = f32[896,128]{1,0:T(8,128)} async-done(((f32[896,128]{1,0:T(8,128)}), f32[896,128]{1,0:T(8,128)}) %all-reduce.5.cloned.1.call-update) | async-done | bytes 458768 | tf_op jit(solution)/shard_map/psum | solution.py:55
  94.8 1.3 %fusion.15 = f32[896,128]{1,0:T(8,128)S(1)} fusion(f32[896,128]{1,0:T(8,128)S(1)} %collective-permute-done, f32[896,128]{1,0:T(8,128)S(1)} %collective-permute-done.2, f32[896,128]{1,0:T(8,128)} %all-reduce.5.cloned.1.call-done, f32[896,128]{1,0:T(8,128)S(1)} %collective-permute-done.1), kind=kLoop, calls=%fused_computation.27 | loop fusion | flops 1490944 | bytes 2293760 | tf_op jit(solution)/shard_map/sub | solution.py:25
  96.1 1.8 %collective-permute-start.3 = (f32[896,128]{1,0:T(8,128)S(1)}, f32[896,128]{1,0:T(8,128)S(1)}, u32[]{:S(2)}, u32[]{:S(2)}) collective-permute-start(f32[896,128]{1,0:T(8,128)S(1)} %fusion.15), channel_id=1, source_target_pairs={{14,0},{0,2},{2,4},{4,6},{6,8},{8,10},{10,12},{12,14},{15,1},{1,3}... | collective-permute-start | bytes 1376264 | tf_op jit(solution)/shard_map/ppermute | solution.py:19
  97.9 5.8 %fusion.9 = f32[2048,128]{1,0:T(8,128)} fusion(f32[2048,128]{1,0:T(8,128)S(1)} %get-tuple-element.7, bf16[2048,896]{1,0:T(8,128)(2,1)} %copy-done.1, f32[2048,128]{1,0:T(8,128)} %get-tuple-element.8, f32[2048,128]{1,0:T(8,128)} %param.11, f32[2048,128]{1,0:T(8,128)} %param.12, f32[896,128]{1,0:T(8,128)S(1)} %collective-permute-done), kind=kOutput, calls=%fused_computation.17 | convolution fusion | flops 475119616 | bytes 9371648 | tf_op jit(solution)/shard_map/dot_general | solution.py:39
  103.7 8.0 %collective-permute-done.3 = f32[896,128]{1,0:T(8,128)S(1)} collective-permute-done((f32[896,128]{1,0:T(8,128)S(1)}, f32[896,128]{1,0:T(8,128)S(1)}, u32[]{:S(2)}, u32[]{:S(2)}) %collective-permute-start.3) | collective-permute-done | bytes 458784 | tf_op jit(solution)/shard_map/ppermute | solution.py:19
  111.7 0.8 copy.35
  (21 shorter events, 0.0 us)
Async XLA Ops:
  7.2 47.1 %all-reduce.3.cloned.1.call-start = ((), (), s32[]{:S(2)}) async-start(), calls=%async_computation | async-start | bytes 917504 | tf_op jit(solution)/shard_map/psum | solution.py:55
  15.1 8.7 %copy-start.2 = (f32[2048,128]{1,0:T(8,128)S(1)}, f32[2048,128]{1,0:T(8,128)}, u32[]{:S(2)}) copy-start(f32[2048,128]{1,0:T(8,128)} %param.10) | copy-start | bytes 3145732
  15.1 8.7 %copy-start.3 = (f32[896,128]{1,0:T(8,128)S(1)}, f32[896,128]{1,0:T(8,128)}, u32[]{:S(2)}) copy-start(f32[896,128]{1,0:T(8,128)} %param.13) | copy-start | bytes 1376260
  29.0 1.8 %copy-start = (bf16[2048,896]{1,0:T(8,128)(2,1)}, bf16[2048,896]{1,0:T(8,128)(2,1)S(1)}, u32[]{:S(2)}) copy-start(bf16[2048,896]{1,0:T(8,128)(2,1)S(1)} %fusion.3) | copy-start | bytes 11010052
  32.8 62.0 %all-reduce.5.cloned.1.call-start = ((), (), s32[]{:S(2)}) async-start(), calls=%async_computation.1 | async-start | bytes 917504 | tf_op jit(solution)/shard_map/psum | solution.py:55
  40.1 14.1 %copy-start.4 = (f32[896,128]{1,0:T(8,128)S(1)}, f32[896,128]{1,0:T(8,128)}, u32[]{:S(2)}) copy-start(f32[896,128]{1,0:T(8,128)} %param.14) | copy-start | bytes 1376260
  40.1 14.1 %copy-start.5 = (f32[896,128]{1,0:T(8,128)S(1)}, f32[896,128]{1,0:T(8,128)}, u32[]{:S(2)}) copy-start(f32[896,128]{1,0:T(8,128)} %param.15) | copy-start | bytes 1376260
  54.2 18.3 %slice-start.2 = ((s8[7340032]{0:T(1024)(128)(4,1)}), s8[4194304]{0:T(1024)(128)(4,1)S(1)}, s32[]{:S(2)}) async-start(s8[7340032]{0:T(1024)(128)(4,1)} %bitcast.34), calls=%async_computation.4 | async-start | bytes 8388608
  56.5 16.0 %slice-start = ((s8[7340032]{0:T(1024)(128)(4,1)}), s8[4194304]{0:T(1024)(128)(4,1)S(1)}, s32[]{:S(2)}) async-start(s8[7340032]{0:T(1024)(128)(4,1)} %bitcast.32), calls=%async_computation.2 | async-start | bytes 8388608
  56.5 16.0 %slice-start.1 = ((s8[7340032]{0:T(1024)(128)(4,1)}), s8[3145728]{0:T(1024)(128)(4,1)S(1)}, s32[]{:S(2)}) async-start(s8[7340032]{0:T(1024)(128)(4,1)} %bitcast.32), calls=%async_computation.3 | async-start | bytes 6291456
  56.5 16.0 %slice-start.3 = ((s8[7340032]{0:T(1024)(128)(4,1)}), s8[3145728]{0:T(1024)(128)(4,1)S(1)}, s32[]{:S(2)}) async-start(s8[7340032]{0:T(1024)(128)(4,1)} %bitcast.34), calls=%async_computation.5 | async-start | bytes 6291456
  56.5 16.0 %collective-permute-start = (f32[896,128]{1,0:T(8,128)S(1)}, f32[896,128]{1,0:T(8,128)S(1)}, u32[]{:S(2)}, u32[]{:S(2)}) collective-permute-start(f32[896,128]{1,0:T(8,128)S(1)} %get-tuple-element.2), channel_id=1, source_target_pairs={{14,0},{0,2},{2,4},{4,6},{6,8},{8,10},{10,12},{12,14},{15,1},{1,3}... | collective-permute-start | bytes 1376264 | tf_op jit(solution)/shard_map/ppermute | solution.py:19
  64.2 18.2 %collective-permute-start.1 = (f32[896,128]{1,0:T(8,128)}, f32[896,128]{1,0:T(8,128)S(1)}, u32[]{:S(2)}, u32[]{:S(2)}) collective-permute-start(f32[896,128]{1,0:T(8,128)} %get-tuple-element.3), channel_id=1, source_target_pairs={{14,0},{0,2},{2,4},{4,6},{6,8},{8,10},{10,12},{12,14},{15,1},{1,3}... | collective-permute-start | bytes 1376264 | tf_op jit(solution)/shard_map/ppermute | solution.py:19
  65.5 26.1 %collective-permute-start.2 = (f32[896,128]{1,0:T(8,128)S(1)}, f32[896,128]{1,0:T(8,128)S(1)}, u32[]{:S(2)}, u32[]{:S(2)}) collective-permute-start(f32[896,128]{1,0:T(8,128)S(1)} %get-tuple-element.4), channel_id=1, source_target_pairs={{14,0},{0,2},{2,4},{4,6},{6,8},{8,10},{10,12},{12,14},{15,1},{1,3}... | collective-permute-start | bytes 1376264 | tf_op jit(solution)/shard_map/ppermute | solution.py:19
  73.8 1.8 %copy-start.1 = (bf16[2048,896]{1,0:T(8,128)(2,1)}, bf16[2048,896]{1,0:T(8,128)(2,1)S(1)}, u32[]{:S(2)}) copy-start(bf16[2048,896]{1,0:T(8,128)(2,1)S(1)} %fusion.1) | copy-start | bytes 11010052
  96.1 15.5 %collective-permute-start.3 = (f32[896,128]{1,0:T(8,128)S(1)}, f32[896,128]{1,0:T(8,128)S(1)}, u32[]{:S(2)}, u32[]{:S(2)}) collective-permute-start(f32[896,128]{1,0:T(8,128)S(1)} %fusion.15), channel_id=1, source_target_pairs={{14,0},{0,2},{2,4},{4,6},{6,8},{8,10},{10,12},{12,14},{15,1},{1,3}... | collective-permute-start | bytes 1376264 | tf_op jit(solution)/shard_map/ppermute | solution.py:19
Sparse Core Ops, SparseCore 0:
  32.9 21.2 all-reduce.2
  77.7 17.1 all-reduce.4
where the time goes:
time: 120 us; the launch traced here: 119 us
  local copies, waits for them, and re-layouts  36.8 us (31%)
  waiting for transfers between devices  36.1 us (30%)
  matrix products  22 us (18%)
  between operations  14.1 us (12%)
  starting transfers between devices  6.64 us (6%)
  other arithmetic  3.59 us (3%)
    ppermute x4, waiting for transfers between devices, passed_along(): return lax.ppermute(block, axis, route)  27.6 us
    mul x4, local copies, waits for them, and re-layouts, residual_grads(): (predict - data.astype(jnp.float32)).reshape(rows // TILE, TILE, cols //...  18.5 us
    unnamed x23, local copies, waits for them, and re-layouts  17.5 us
    dot_general x2, matrix products, residual_grads(): grad_sys = jnp.dot(error, time_low, preferred_element_type=jnp.float32)  11.7 us
    psum x2, waiting for transfers between devices, on_device(): grad_time = lax.psum(part_time, 'rep')  8.53 us
    dot_general x2, matrix products, residual_grads(): predict = jnp.dot(sys_low, time_low.T, preferred_element_type=jnp.float32)  6.45 us
    ppermute x4, starting transfers between devices, passed_along(): return lax.ppermute(block, axis, route)  6.38 us
    dot_general x2, matrix products, residual_grads(): lax.dot_general(error, sys_low, (((0,), (0,)), ((), ())), preferred_eleme...  3.88 us
  transfers between devices with their start and end apart: 6, of which 6 were waited for; matrix products, arithmetic and copies ran while one was open for 26% of the time, Pallas kernels for 0%

commit v1 on v0

v1 whole, which is shorter than its diff:
```python
import functools

import jax
import jax.numpy as jnp
from jax import lax
from jax.experimental import pallas as pl
from jax.experimental.pallas import tpu as pltpu
from jax.sharding import PartitionSpec as P

TILE = 128
CHUNK = 256
ROWS = 256
MESH = pl.DeviceIdType.MESH

learn_rate = 0.1
beta_one = 0.8
beta_two = 0.99
adam_eps = 1e-08
decay_weight = 0.01


def adam_step(param, first, second, grad):
    first_new = beta_one * first + (1.0 - beta_one) * grad
    second_new = beta_two * second + (1.0 - beta_two) * grad * grad
    param_new = param - learn_rate * first_new / (jnp.sqrt(second_new) + adam_eps)
    return (param_new, first_new, second_new)


def kernel(
    n_blk, chunks,
    data_hbm, mask_ref, u_hbm, um_hbm, uv_hbm, h_hbm, hm_hbm, hv_hbm,
    u_out, h_out,
    data, u, um, uv, ub, err, h, hm, hv, hn, hb, part, px, gb, gr, mx, h2,
    in_sem, data_sem, out_sem,
    x_send, x_recv, h_send, h_recv, f_send, f_recv, g_send, g_recv,
    m_send, m_recv, o_send, o_recv, p_send, p_recv, q_send, q_recv,
):
    systems = u.shape[0]
    count = len(chunks)
    last = count - 1
    me = lax.axis_index("blk")
    core = lax.axis_index("rep")
    other = 1 - core
    after, before = lax.rem(me + 1, n_blk), lax.rem(me + n_blk - 1, n_blk)
    after2, before2 = lax.rem(me + 2, n_blk), lax.rem(me + n_blk - 2, n_blk)

    barrier = pltpu.get_barrier_semaphore()
    friends = [
        {"rep": other},
        {"blk": after}, {"blk": after, "rep": other},
        {"blk": before}, {"blk": before, "rep": other},
        {"blk": after2}, {"blk": before2},
    ]
    for friend in friends:
        pl.semaphore_signal(barrier, inc=1, device_id=friend, device_id_type=MESH)

    def fetch(src, dst, k):
        return pltpu.make_async_copy(src, dst, in_sem.at[k])

    in_h, in_u = fetch(h_hbm, h, 0), fetch(u_hbm, u, 1)
    in_hm, in_hv = fetch(hm_hbm, hm, 2), fetch(hv_hbm, hv, 3)
    in_um, in_uv = fetch(um_hbm, um, 4), fetch(uv_hbm, uv, 5)
    in_data = [
        [
            pltpu.make_async_copy(
                data_hbm.at[s, :, pl.ds(off, w)], data.at[s, :, pl.ds(off, w)], data_sem.at[s, c]
            )
            for c, (off, w) in enumerate(chunks)
        ]
        for s in range(2)
    ]
    in_h.start()
    in_u.start()
    for c in range(count):
        in_data[0][c].start()
        if c == 0:
            in_hm.start()
            in_hv.start()
    in_um.start()
    in_uv.start()
    for c in range(count):
        in_data[1][c].start()

    def remote(src, dst, send, recv, device):
        return pltpu.make_async_remote_copy(
            src_ref=src, dst_ref=dst, send_sem=send, recv_sem=recv,
            device_id=device, device_id_type=MESH,
        )

    def rows_of(c, which):
        off, w = chunks[c]
        return pl.ds(pl.multiple_of(off + which * (w // 2), w // 2), w // 2)

    def half_of(c):
        off, w = chunks[c]
        return pl.ds(off // 2, w // 2)

    swap = [
        [
            remote(part.at[s, rows_of(c, other)], px.at[s, half_of(c)],
                   x_send.at[s, c], x_recv.at[s, c], {"rep": other})
            for c in range(count)
        ]
        for s in range(2)
    ]
    pass_h = [
        remote(h.at[rows_of(c, core)], hn.at[rows_of(c, core)], h_send.at[c], h_recv.at[c], {"blk": after})
        for c in range(count)
    ]
    share_h = [
        remote(hn.at[rows_of(c, core)], hn.at[rows_of(c, core)], f_send.at[c], f_recv.at[c], {"rep": other})
        for c in range(count)
    ]
    back = [
        remote(gb.at[half_of(c)], gr.at[half_of(c)], g_send.at[c], g_recv.at[c], {"blk": before})
        for c in range(last)
    ]
    final = [
        remote(h2.at[half_of(c)], h_out.at[rows_of(c, core)], o_send.at[c], o_recv.at[c],
               {"blk": after if c == last else after2})
        for c in range(count)
    ]
    share_out = [
        remote(h_out.at[rows_of(c, core)], h_out.at[rows_of(c, core)], p_send.at[c], p_recv.at[c], {"rep": other})
        for c in range(last)
    ]
    final_two = remote(
        h2.at[half_of(last)], h_out.at[rows_of(last, core)], q_send, q_recv, {"blk": after, "rep": other}
    )
    pass_m = [
        remote(src.at[rows_of(last, core)], mx.at[k], m_send.at[k], m_recv.at[k], {"blk": after})
        for k, src in enumerate((hm, hv))
    ]

    def grads(s, c):
        off, w = chunks[c]

        def block(i):
            rows = pl.ds(pl.multiple_of(i * ROWS, ROWS), ROWS)
            predict = lax.dot_general(
                ub[rows, :], hb[off : off + w, :], (((1,), (1,)), ((), ())),
                preferred_element_type=jnp.float32,
            )
            diff = predict - data[s, rows, off : off + w].astype(jnp.float32)
            for a in range(ROWS // TILE):
                for b in range(w // TILE):
                    keep = mask_ref[s, i * (ROWS // TILE) + a, off // TILE + b].astype(jnp.float32)
                    piece = diff[a * TILE : (a + 1) * TILE, b * TILE : (b + 1) * TILE] * keep
                    err[
                        pl.ds(pl.multiple_of(i * ROWS + a * TILE, TILE), TILE),
                        off + b * TILE : off + (b + 1) * TILE,
                    ] = piece.astype(jnp.bfloat16)

        def pair(i, carry):
            block(2 * i)
            block(2 * i + 1)
            return carry

        lax.fori_loop(0, systems // ROWS // 2, pair, 0)
        part[s, off : off + w, :] = lax.dot_general(
            err[:, off : off + w], ub[...], (((0,), (0,)), ((), ())),
            preferred_element_type=jnp.float32,
        )

    def sys_block(s, i):
        rows = pl.ds(pl.multiple_of(i * ROWS, ROWS), ROWS)
        grad = jnp.dot(err[rows, :], hb[...], preferred_element_type=jnp.float32)
        param = u[rows, :]
        new, one, two = adam_step(param, um[rows, :], uv[rows, :], grad + decay_weight * param)
        u[rows, :] = new
        if s == 0:
            um[rows, :] = one
            uv[rows, :] = two
            ub[rows, :] = new.astype(jnp.bfloat16)

    pieces = 4
    per = systems // pieces

    def sys_piece(s, p):
        for i in range(p * per // ROWS, (p + 1) * per // ROWS):
            sys_block(s, i)

    out_copy = [
        pltpu.make_async_copy(u.at[pl.ds(p * per, per)], u_out.at[pl.ds(p * per, per)], out_sem.at[p])
        for p in range(pieces)
    ]

    def home_first(c):
        swap[0][c].wait_recv()
        rows = rows_of(c, core)
        param = h[rows, :]
        grad = part[0, rows, :] + px[0, half_of(c), :] + decay_weight * param
        new, one, two = adam_step(param, hm[rows, :], hv[rows, :], grad)
        h[rows, :] = new
        hm[rows, :] = one
        hv[rows, :] = two
        pass_h[c].start()
        if c == last:
            for copy in pass_m:
                copy.start()

    def hand_on(c):
        pass_h[c].wait_recv()
        share_h[c].start()

    def give_back(c):
        swap[1][c].wait_recv()
        rows = rows_of(c, core)
        gb[half_of(c), :] = part[1, rows, :] + px[1, half_of(c), :]
        back[c].start()

    def home_second(c):
        back[c].wait_recv()
        rows = rows_of(c, core)
        param = h[rows, :]
        grad = gr[half_of(c), :] + decay_weight * param
        h2[half_of(c), :] = adam_step(param, hm[rows, :], hv[rows, :], grad)[0]
        final[c].start()

    def finish_last():
        for copy in pass_m:
            copy.wait_recv()
        swap[1][last].wait_recv()
        rows = rows_of(last, core)
        param = hn[rows, :]
        grad = part[1, rows, :] + px[1, half_of(last), :] + decay_weight * param
        h2[half_of(last), :] = adam_step(param, mx[0], mx[1], grad)[0]
        final[last].start()
        final_two.start()

    def share_final(c):
        final[c].wait_recv()
        share_out[c].start()

    in_h.wait()
    hb[...] = h[...].astype(jnp.bfloat16)
    in_u.wait()
    ub[...] = u[...].astype(jnp.bfloat16)
    for c in range(count):
        in_data[0][c].wait()
        grads(0, c)
        if c == 0:
            pl.semaphore_wait(barrier, len(friends))
            in_hm.wait()
            in_hv.wait()
        swap[0][c].start()
        if c >= 1:
            home_first(c - 1)
    in_um.wait()
    in_uv.wait()
    sys_piece(0, 0)
    home_first(last)
    for p in range(1, pieces):
        hand_on(p - 1)
        sys_piece(0, p)
    for c in range(pieces - 1, count):
        hand_on(c)

    for c, (off, w) in enumerate(chunks):
        in_data[1][c].wait()
        share_h[c].wait_recv()
        hb[off : off + w, :] = hn[off : off + w, :].astype(jnp.bfloat16)
        grads(1, c)
        swap[1][c].start()
        if c >= 1:
            give_back(c - 1)
        if c >= 2:
            home_second(c - 2)
    sys_piece(1, 0)
    out_copy[0].start()
    finish_last()
    home_second(last - 1)
    for p in range(1, pieces):
        sys_piece(1, p)
        out_copy[p].start()
        if p <= last:
            share_final(p - 1)
    for c in range(pieces - 1, last):
        share_final(c)

    for s in range(2):
        for c in range(count):
            swap[s][c].wait_send()
    for group in (pass_h, share_h, back, final, share_out, pass_m, [final_two]):
        for copy in group:
            copy.wait_send()
    for copy in share_out:
        copy.wait_recv()
    final[last].wait_recv()
    final_two.wait_recv()
    for copy in out_copy:
        copy.wait()


def on_device(
    readings, tile_mask, sys_factors, sys_first, sys_second, time_factors, time_first, time_second
):
    n_blk = lax.axis_size("blk")
    systems, rank = sys_factors.shape
    times = time_factors.shape[0]
    chunks = tuple((off, min(CHUNK, times - off)) for off in range(0, times, CHUNK))
    count = len(chunks)
    f32, bf16 = jnp.float32, jnp.bfloat16
    dma = pltpu.SemaphoreType.DMA
    anywhere = pl.BlockSpec(memory_space=pl.ANY)
    small = chunks[-1][1] // 2
    return pl.pallas_call(
        functools.partial(kernel, n_blk, chunks),
        out_shape=(
            jax.ShapeDtypeStruct((systems, rank), f32),
            jax.ShapeDtypeStruct((times, rank), f32),
        ),
        in_specs=[anywhere, pl.BlockSpec(memory_space=pltpu.SMEM)] + [anywhere] * 6,
        out_specs=(anywhere, anywhere),
        scratch_shapes=[
            pltpu.VMEM((2, systems, times), bf16),
            pltpu.VMEM((systems, rank), f32),
            pltpu.VMEM((systems, rank), f32),
            pltpu.VMEM((systems, rank), f32),
            pltpu.VMEM((systems, rank), bf16),
            pltpu.VMEM((systems, times), bf16),
            pltpu.VMEM((times, rank), f32),
            pltpu.VMEM((times, rank), f32),
            pltpu.VMEM((times, rank), f32),
            pltpu.VMEM((times, rank), f32),
            pltpu.VMEM((times, rank), bf16),
            pltpu.VMEM((2, times, rank), f32),
            pltpu.VMEM((2, times // 2, rank), f32),
            pltpu.VMEM((times // 2, rank), f32),
            pltpu.VMEM((times // 2, rank), f32),
            pltpu.VMEM((2, small, rank), f32),
            pltpu.VMEM((times // 2, rank), f32),
            dma((6,)), dma((2, count)), dma((4,)),
            dma((2, count)), dma((2, count)),
            dma((count,)), dma((count,)),
            dma((count,)), dma((count,)),
            dma((count,)), dma((count,)),
            dma((2,)), dma((2,)),
            dma((count,)), dma((count,)),
            dma((count,)), dma((count,)),
            dma, dma,
        ],
        compiler_params=pltpu.CompilerParams(
            collective_id=0, has_side_effects=True, vmem_limit_bytes=56 * 1024 * 1024
        ),
    )(readings, tile_mask, sys_factors, sys_first, sys_second, time_factors, time_first, time_second)


def solution(mesh):
    return jax.shard_map(
        on_device,
        mesh=mesh,
        in_specs=(
            P(None, ("region", "blk", "rep"), None),
            P(None, ("region", "blk", "rep"), None),
            P(("region", "blk", "rep"), None),
            P(("region", "blk", "rep"), None),
            P(("region", "blk", "rep"), None),
            P(("region", "blk"), None),
            P(("region", "blk"), None),
            P(("region", "blk"), None),
        ),
        out_specs=(P(("region", "blk", "rep"), None), P(("region", "blk"), None)),
        check_vma=False,
    )
```

time: 120 us -> 44.2 us (0.37)
  Pallas kernels: 0 us -> 37.8 us
  waiting for transfers between devices: 36.1 us -> 0 us
  local copies, waits for them, and re-layouts: 36.8 us -> 5.46 us
  matrix products: 22 us -> 0 us
  between operations: 14.1 us -> 0.64 us
  starting transfers between devices: 6.64 us -> 0 us
  other arithmetic: 3.59 us -> 0 us
    pallas_call x0 -> x1, Pallas kernels: none -> 37.8 us  [on_device(): pl.pallas_call(functools.partial(kernel, n_blk, chunks), out_shape=(jax.S...]
    ppermute x4 -> x0, waiting for transfers between devices: 27.6 us -> none  [passed_along(): return lax.ppermute(block, axis, route)]
    dot_general x6 -> x0, matrix products: 22 us -> none  [the longest x2 11.7 us: residual_grads(): grad_sys = jnp.dot(error, time_low, preferred_element_type=jnp.float32)]
    mul x4 -> x0, local copies, waits for them, and re-layouts: 18.5 us -> none  [residual_grads(): (predict - data.astype(jnp.float32)).reshape(rows // TILE, TILE, cols //...]
    unnamed x23 -> x3, local copies, waits for them, and re-layouts: 17.5 us -> 5.46 us
    psum x2 -> x0, waiting for transfers between devices: 8.53 us -> none  [on_device(): grad_time = lax.psum(part_time, 'rep')]
    ppermute x4 -> x0, starting transfers between devices: 6.38 us -> none  [passed_along(): return lax.ppermute(block, axis, route)]
    sub x2 -> x0, other arithmetic: 3.58 us -> none  [adam_step(): param - learn_rate * first_new / (jnp.sqrt(second_new) + adam_eps)]
  transfers between devices with their start and end apart: 6 -> 0, of which waited for: 6 -> 0; matrix products, arithmetic and copies ran while one was open for 26% -> 0% of each run, Pallas kernels for 0% -> 0%
where the time goes in v1:
time: 44.2 us; the launch traced here: 43.9 us
  Pallas kernels  37.8 us (86%)
  local copies, waits for them, and re-layouts  5.46 us (12%)
  between operations  0.64 us (1%)
    pallas_call x1, Pallas kernels, on_device(): pl.pallas_call(functools.partial(kernel, n_blk, chunks), out_shape=(jax.S...  37.8 us
    unnamed x3, local copies, waits for them, and re-layouts  5.46 us

profile of v1, /device:TPU:0, one launch (start us, length us, event | category | flops | bytes accessed | tf_op | source)
XLA Modules:
  0.0 43.9 jit_solution(18260984714393162545)
XLA Ops:
  0.6 1.4 %copy.10.mask_ref = s32[2,16,7]{2,1,0:T(8,128)} copy(s32[2,16,7]{1,0,2:T(2,128)} %param.9) | data formatting | bytes 1792 | tf_op args[1]
  2.0 37.8 %shard_map.95 = (f32[2048,128]{1,0:T(8,128)}, f32[896,128]{1,0:T(8,128)}) custom-call(bf16[2,2048,896]{2,1,0:T(8,128)(2,1)} %data_hbm.1, s32[2,16,7]{2,1,0:T(8,128)} %copy.10.mask_ref, f32[2048,128]{1,0:T(8,128)} %u_hbm.1, f32[2048,128]{1,0:T(8,128)} %um_hbm.1, f32[2048,128]{1,0:T(8,128)} %uv_hbm.1, f32[896,128]{1,0:T(8,128)} %h_hbm.1, f32[896,128]{1,0:T(8,128)} %hm_hbm.1, ...), custom_call_target="tpu_custom_call" | custom-call | tf_op jit(solution)/shard_map/pallas_call | solution.py:307
  39.8 2.3 %copy.13 = f32[2048,128]{1,0:T(8,128)} copy(f32[2048,128]{1,0:T(8,128)} %get-tuple-element.4) | data formatting | bytes 2097152
  42.1 1.8 %copy.14 = f32[896,128]{1,0:T(8,128)} copy(f32[896,128]{1,0:T(8,128)} %get-tuple-element.5) | data formatting | bytes 917504

commit v2 on v1

--- a/solution.py
+++ b/solution.py
@@ -9,6 +9,7 @@
 
 TILE = 128
 CHUNK = 256
+HOME = ()
 ROWS = 256
 MESH = pl.DeviceIdType.MESH
 
@@ -30,8 +31,8 @@
     n_blk, chunks,
     data_hbm, mask_ref, u_hbm, um_hbm, uv_hbm, h_hbm, hm_hbm, hv_hbm,
     u_out, h_out,
-    data, u, um, uv, ub, err, h, hm, hv, hn, hb, part, px, gb, gr, mx, h2,
-    in_sem, data_sem, out_sem,
+    data, u, um, uv, ub, err, h, hm, hv, hn, hb, part, px, gb, gr, mx, h2, ho,
+    in_sem, data_sem, out_sem, ho_sem,
     x_send, x_recv, h_send, h_recv, f_send, f_recv, g_send, g_recv,
     m_send, m_recv, o_send, o_recv, p_send, p_recv, q_send, q_recv,
 ):
@@ -113,24 +114,28 @@
     ]
     back = [
         remote(gb.at[half_of(c)], gr.at[half_of(c)], g_send.at[c], g_recv.at[c], {"blk": before})
-        for c in range(last)
+        for c in range(count)
     ]
     final = [
-        remote(h2.at[half_of(c)], h_out.at[rows_of(c, core)], o_send.at[c], o_recv.at[c],
-               {"blk": after if c == last else after2})
+        remote(h2.at[half_of(c)], (h_out if c == last else ho).at[rows_of(c, core)], o_send.at[c], o_recv.at[c],
+               {"blk": after2 if c in HOME else after})
         for c in range(count)
     ]
     share_out = [
-        remote(h_out.at[rows_of(c, core)], h_out.at[rows_of(c, core)], p_send.at[c], p_recv.at[c], {"rep": other})
+        remote(ho.at[rows_of(c, core)], ho.at[rows_of(c, core)], p_send.at[c], p_recv.at[c], {"rep": other})
         for c in range(last)
     ]
     final_two = remote(
         h2.at[half_of(last)], h_out.at[rows_of(last, core)], q_send, q_recv, {"blk": after, "rep": other}
     )
     pass_m = [
-        remote(src.at[rows_of(last, core)], mx.at[k], m_send.at[k], m_recv.at[k], {"blk": after})
-        for k, src in enumerate((hm, hv))
-    ]
+        [
+            remote(src.at[rows_of(c, core)], mx.at[k, half_of(c)], m_send.at[k, c], m_recv.at[k, c], {"blk": after})
+            for k, src in enumerate((hm, hv))
+        ]
+        for c in range(count)
+    ]
+    travel = [c for c in range(count) if c not in HOME]
 
     def grads(s, c):
         off, w = chunks[c]
@@ -144,7 +149,7 @@
             diff = predict - data[s, rows, off : off + w].astype(jnp.float32)
             for a in range(ROWS // TILE):
                 for b in range(w // TILE):
-                    keep = mask_ref[s, i * (ROWS // TILE) + a, off // TILE + b].astype(jnp.float32)
+                    keep = mask_ref[off // TILE + b, s, i * (ROWS // TILE) + a].astype(jnp.float32)
                     piece = diff[a * TILE : (a + 1) * TILE, b * TILE : (b + 1) * TILE] * keep
                     err[
                         pl.ds(pl.multiple_of(i * ROWS + a * TILE, TILE), TILE),
@@ -183,6 +188,11 @@
     out_copy = [
         pltpu.make_async_copy(u.at[pl.ds(p * per, per)], u_out.at[pl.ds(p * per, per)], out_sem.at[p])
         for p in range(pieces)
+    ]
+
+    ho_copy = [
+        pltpu.make_async_copy(ho.at[pl.ds(off, w)], h_out.at[pl.ds(off, w)], ho_sem.at[c])
+        for c, (off, w) in enumerate(chunks[:last])
     ]
 
     def home_first(c):
@@ -196,8 +206,9 @@
         hv[rows, :] = two
         pass_h[c].start()
         if c == last:
-            for copy in pass_m:
-                copy.start()
+            for k in travel:
+                for copy in pass_m[k]:
+                    copy.start()
 
     def hand_on(c):
         pass_h[c].wait_recv()
@@ -217,16 +228,17 @@
         h2[half_of(c), :] = adam_step(param, hm[rows, :], hv[rows, :], grad)[0]
         final[c].start()
 
-    def finish_last():
-        for copy in pass_m:
+    def finish(c):
+        for copy in pass_m[c]:
             copy.wait_recv()
-        swap[1][last].wait_recv()
-        rows = rows_of(last, core)
+        swap[1][c].wait_recv()
+        rows = rows_of(c, core)
         param = hn[rows, :]
-        grad = part[1, rows, :] + px[1, half_of(last), :] + decay_weight * param
-        h2[half_of(last), :] = adam_step(param, mx[0], mx[1], grad)[0]
-        final[last].start()
-        final_two.start()
+        grad = part[1, rows, :] + px[1, half_of(c), :] + decay_weight * param
+        h2[half_of(c), :] = adam_step(param, mx[0, half_of(c), :], mx[1, half_of(c), :], grad)[0]
+        final[c].start()
+        if c == last:
+            final_two.start()
 
     def share_final(c):
         final[c].wait_recv()
@@ -251,45 +263,83 @@
     sys_piece(0, 0)
     home_first(last)
     for p in range(1, pieces):
-        hand_on(p - 1)
         sys_piece(0, p)
-    for c in range(pieces - 1, count):
-        hand_on(c)
+    hand_on(0)
 
     for c, (off, w) in enumerate(chunks):
+        if c < last:
+            hand_on(c + 1)
         in_data[1][c].wait()
         share_h[c].wait_recv()
         hb[off : off + w, :] = hn[off : off + w, :].astype(jnp.bfloat16)
         grads(1, c)
         swap[1][c].start()
         if c >= 1:
-            give_back(c - 1)
-        if c >= 2:
-            home_second(c - 2)
+            give_back(c - 1) if c - 1 in HOME else finish(c - 1)
     sys_piece(1, 0)
     out_copy[0].start()
-    finish_last()
-    home_second(last - 1)
+    finish(last)
+    for c in HOME:
+        home_second(c)
     for p in range(1, pieces):
         sys_piece(1, p)
         out_copy[p].start()
-        if p <= last:
-            share_final(p - 1)
-    for c in range(pieces - 1, last):
+    for c in range(last):
         share_final(c)
 
+    for c in range(last):
+        share_out[c].wait_recv()
+        ho_copy[c].start()
     for s in range(2):
         for c in range(count):
             swap[s][c].wait_send()
-    for group in (pass_h, share_h, back, final, share_out, pass_m, [final_two]):
+    for group in (pass_h, share_h, final, share_out, [final_two]):
         for copy in group:
             copy.wait_send()
-    for copy in share_out:
-        copy.wait_recv()
+    for c in range(count):
+        for copy in [back[c]] if c in HOME else pass_m[c]:
+            copy.wait_send()
     final[last].wait_recv()
     final_two.wait_recv()
-    for copy in out_copy:
+    for copy in out_copy + ho_copy:
         copy.wait()
+
+
+def place_kernel(u_in, h_in, u_to, h_to, u_mid, h_mid, read_sem, write_sem):
+    per = u_in.shape[0] // 4
+    moves = [(h_in, h_mid, h_to, pl.ds(0, h_in.shape[0]))] + [
+        (u_in, u_mid, u_to, pl.ds(k * per, per)) for k in range(4)
+    ]
+    reads = [
+        pltpu.make_async_copy(src.at[rows], mid.at[rows], read_sem.at[k])
+        for k, (src, mid, _, rows) in enumerate(moves)
+    ]
+    writes = [
+        pltpu.make_async_copy(mid.at[rows], dst.at[rows], write_sem.at[k])
+        for k, (_, mid, dst, rows) in enumerate(moves)
+    ]
+    for read in reads:
+        read.start()
+    for read, write in zip(reads, writes):
+        read.wait()
+        write.start()
+    for write in writes:
+        write.wait()
+
+
+def placed(u, h):
+    anywhere = pl.BlockSpec(memory_space=pl.ANY)
+    return pl.pallas_call(
+        place_kernel,
+        out_shape=(jax.ShapeDtypeStruct(u.shape, u.dtype), jax.ShapeDtypeStruct(h.shape, h.dtype)),
+        in_specs=[anywhere, anywhere],
+        out_specs=(anywhere, anywhere),
+        scratch_shapes=[
+            pltpu.VMEM(u.shape, u.dtype), pltpu.VMEM(h.shape, h.dtype),
+            pltpu.SemaphoreType.DMA((5,)), pltpu.SemaphoreType.DMA((5,)),
+        ],
+        compiler_params=pltpu.CompilerParams(vmem_limit_bytes=56 * 1024 * 1024),
+    )(u, h)
 
 
 def on_device(
@@ -303,8 +353,7 @@
     f32, bf16 = jnp.float32, jnp.bfloat16
     dma = pltpu.SemaphoreType.DMA
     anywhere = pl.BlockSpec(memory_space=pl.ANY)
-    small = chunks[-1][1] // 2
-    return pl.pallas_call(
+    results = pl.pallas_call(
         functools.partial(kernel, n_blk, chunks),
         out_shape=(
             jax.ShapeDtypeStruct((systems, rank), f32),
@@ -328,14 +377,15 @@
             pltpu.VMEM((2, times // 2, rank), f32),
             pltpu.VMEM((times // 2, rank), f32),
             pltpu.VMEM((times // 2, rank), f32),
-            pltpu.VMEM((2, small, rank), f32),
+            pltpu.VMEM((2, times // 2, rank), f32),
             pltpu.VMEM((times // 2, rank), f32),
-            dma((6,)), dma((2, count)), dma((4,)),
+            pltpu.VMEM((times, rank), f32),
+            dma((6,)), dma((2, count)), dma((4,)), dma((count,)),
             dma((2, count)), dma((2, count)),
             dma((count,)), dma((count,)),
             dma((count,)), dma((count,)),
             dma((count,)), dma((count,)),
-            dma((2,)), dma((2,)),
+            dma((2, count)), dma((2, count)),
             dma((count,)), dma((count,)),
             dma((count,)), dma((count,)),
             dma, dma,
@@ -343,7 +393,8 @@
         compiler_params=pltpu.CompilerParams(
             collective_id=0, has_side_effects=True, vmem_limit_bytes=56 * 1024 * 1024
         ),
-    )(readings, tile_mask, sys_factors, sys_first, sys_second, time_factors, time_first, time_second)
+    )(readings, jnp.transpose(tile_mask, (2, 0, 1)), sys_factors, sys_first, sys_second, time_factors, time_first, time_second)
+    return placed(*results)
 
 
 def solution(mesh):

time: 44.2 us -> 38 us (0.86); the launches traced: 43.9 us -> 37.2 us
  local copies, waits for them, and re-layouts: 5.46 us -> 0 us
  Pallas kernels: 37.8 us -> 36.6 us
    unnamed x3 -> x0, local copies, waits for them, and re-layouts: 5.46 us -> none
    pallas_call x1, Pallas kernels: 37.8 us -> 34.4 us  [on_device(): pl.pallas_call(functools.partial(kernel, n_blk, chunks), out_shape=(jax.S...]
    pallas_call x0 -> x1, Pallas kernels: none -> 2.22 us  [placed(): pl.pallas_call(place_kernel, out_shape=(jax.ShapeDtypeStruct(u.shape, u.d...]
where the time goes in v2:
time: 38 us; the launch traced here: 37.2 us
  Pallas kernels  36.6 us (96%)
  between operations  0.64 us (2%)
    pallas_call x1, Pallas kernels, on_device(): pl.pallas_call(functools.partial(kernel, n_blk, chunks), out_shape=(jax.S...  34.4 us
    pallas_call x1, Pallas kernels, placed(): pl.pallas_call(place_kernel, out_shape=(jax.ShapeDtypeStruct(u.shape, u.d...  2.22 us

profile of v2, /device:TPU:0, one launch (start us, length us, event | category | flops | bytes accessed | tf_op | source)
XLA Modules:
  0.0 37.2 jit_solution(17358862316719241487)
XLA Ops:
  0.6 34.4 %shard_map.95 = (f32[2048,128]{1,0:T(8,128)}, f32[896,128]{1,0:T(8,128)}) custom-call(bf16[2,2048,896]{2,1,0:T(8,128)(2,1)} %data_hbm.1, s32[7,2,16]{2,1,0:T(2,128)} %bitcast.1, f32[2048,128]{1,0:T(8,128)} %u_hbm.1, f32[2048,128]{1,0:T(8,128)} %um_hbm.1, f32[2048,128]{1,0:T(8,128)} %uv_hbm.1, f32[896,128]{1,0:T(8,128)} %h_hbm.1, f32[896,128]{1,0:T(8,128)} %hm_hbm.1, ...), custom_call_target="tpu_custom_call" | custom-call | tf_op jit(solution)/shard_map/pallas_call | solution.py:356
  35.0 2.2 %shard_map.96 = (f32[2048,128]{1,0:T(8,128)}, f32[896,128]{1,0:T(8,128)}) custom-call(f32[2048,128]{1,0:T(8,128)} %get-tuple-element.4.u_in, f32[896,128]{1,0:T(8,128)} %get-tuple-element.5.h_in), custom_call_target="tpu_custom_call" | custom-call | tf_op jit(solution)/shard_map/pallas_call | solution.py:332

commit v3 on v2

--- a/solution.py
+++ b/solution.py
@@ -122,7 +122,7 @@
         for c in range(count)
     ]
     share_out = [
-        remote(ho.at[rows_of(c, core)], ho.at[rows_of(c, core)], p_send.at[c], p_recv.at[c], {"rep": other})
+        remote(ho.at[rows_of(c, core)], h_out.at[rows_of(c, core)], p_send.at[c], p_recv.at[c], {"rep": other})
         for c in range(last)
     ]
     final_two = remote(
@@ -191,8 +191,8 @@
     ]
 
     ho_copy = [
-        pltpu.make_async_copy(ho.at[pl.ds(off, w)], h_out.at[pl.ds(off, w)], ho_sem.at[c])
-        for c, (off, w) in enumerate(chunks[:last])
+        pltpu.make_async_copy(ho.at[rows_of(c, core)], h_out.at[rows_of(c, core)], ho_sem.at[c])
+        for c in range(last)
     ]
 
     def home_first(c):
@@ -243,6 +243,7 @@
     def share_final(c):
         final[c].wait_recv()
         share_out[c].start()
+        ho_copy[c].start()
 
     in_h.wait()
     hb[...] = h[...].astype(jnp.bfloat16)
@@ -289,7 +290,6 @@
 
     for c in range(last):
         share_out[c].wait_recv()
-        ho_copy[c].start()
     for s in range(2):
         for c in range(count):
             swap[s][c].wait_send()

time: 38 us -> 37.6 us (0.989); the launches traced: 37.2 us -> 37.4 us
  no operation moved by 1% of the time
where the time goes in v3:
time: 37.6 us; the launch traced here: 37.4 us
  Pallas kernels  36.7 us (98%)
  between operations  0.64 us (2%)
    pallas_call x1, Pallas kernels, on_device(): pl.pallas_call(functools.partial(kernel, n_blk, chunks), out_shape=(jax.S...  34.5 us
    pallas_call x1, Pallas kernels, placed(): pl.pallas_call(place_kernel, out_shape=(jax.ShapeDtypeStruct(u.shape, u.d...  2.22 us

profile of v3, /device:TPU:0, one launch (start us, length us, event | category | flops | bytes accessed | tf_op | source)
XLA Modules:
  0.0 37.4 jit_solution(12641130000603454427)
XLA Ops:
  0.6 34.5 %shard_map.95 = (f32[2048,128]{1,0:T(8,128)}, f32[896,128]{1,0:T(8,128)}) custom-call(bf16[2,2048,896]{2,1,0:T(8,128)(2,1)} %data_hbm.1, s32[7,2,16]{2,1,0:T(2,128)} %bitcast.1, f32[2048,128]{1,0:T(8,128)} %u_hbm.1, f32[2048,128]{1,0:T(8,128)} %um_hbm.1, f32[2048,128]{1,0:T(8,128)} %uv_hbm.1, f32[896,128]{1,0:T(8,128)} %h_hbm.1, f32[896,128]{1,0:T(8,128)} %hm_hbm.1, ...), custom_call_target="tpu_custom_call" | custom-call | tf_op jit(solution)/shard_map/pallas_call | solution.py:356
  35.1 2.2 %shard_map.96 = (f32[2048,128]{1,0:T(8,128)}, f32[896,128]{1,0:T(8,128)}) custom-call(f32[2048,128]{1,0:T(8,128)} %get-tuple-element.4.u_in, f32[896,128]{1,0:T(8,128)} %get-tuple-element.5.h_in), custom_call_target="tpu_custom_call" | custom-call | tf_op jit(solution)/shard_map/pallas_call | solution.py:332
